TPU v7x, 32 devices: a whole 2x2x4 slice. The times are simulated.
32 devices in a mesh: groups: 2 (over y), dp: 8 (over z, x), tensor: 2 (over core).
Axes of the slice: x: 2, y: 2, z: 4, core: 2. Of those that a mesh axis runs over, the one named last changes fastest.
Arguments:
- train_inputs: bfloat16 [64, 32, 14336], P(('groups', 'dp'), None, 'tensor'), parts along dimension 0, may hold values from -6 to 6
- train_grads: bfloat16 [64, 32, 8192], P(('groups', 'dp'), None, 'tensor'), parts along dimension 0, may hold values from -6 to 6
- train_lengths: int32 [64], P(('groups', 'dp')), parts along dimension 0, may hold values from 4 to 32
- query_inputs: bfloat16 [48, 32, 14336], P(('groups', 'dp'), None, 'tensor'), parts along dimension 0, may hold values from -6 to 6
- query_grads: bfloat16 [48, 32, 8192], P(('groups', 'dp'), None, 'tensor'), parts along dimension 0, may hold values from -6 to 6
- query_lengths: int32 [48], P(('groups', 'dp')), parts along dimension 0, may hold values from 4 to 32
- proj_in: bfloat16 [2, 64, 7168], P('tensor', None, 'dp'), may hold values from -0.046875 to 0.046875
- proj_out: bfloat16 [2, 64, 4096], P('tensor', None, 'dp'), may hold values from -0.0625 to 0.0625
Outputs:
- scores: float32 [64, 24], P(('groups', 'dp', 'tensor')), parts along dimension 0
There are 2 independent parts, one for each index of `groups`. A program takes and returns all parts, laid end to end along the dimension named above; an argument that names none is the same for every part. Nothing has to cross between parts.
All inputs are finite; a program needn't handle non-finite values.
Results may differ from a plain program's by a relative error of at most 0.015.
Values may be sent and summed in bfloat16 or wider, within the bound.
A program may use at most 64 MiB of HBM per device.

v0:
```python
import jax
import jax.numpy as jnp
from jax import lax
from jax.sharding import PartitionSpec as P


def project_tokens(inputs, grads, proj_in, proj_out):
    count = inputs.shape[0] * inputs.shape[1]
    in_side = lax.dot_general(
        inputs.reshape(count, inputs.shape[2]),
        proj_in,
        (((1,), (1,)), ((), ())),
        preferred_element_type=jnp.float32,
    )
    out_side = lax.dot_general(
        grads.reshape(count, grads.shape[2]),
        proj_out,
        (((1,), (1,)), ((), ())),
        preferred_element_type=jnp.float32,
    )
    joined = jnp.concatenate([in_side, out_side], axis=1)
    return joined.reshape(inputs.shape[0], inputs.shape[1], joined.shape[1])


def seq_gradient(projected, lengths, row_count):
    proj_rank = projected.shape[2] // 2
    seq_len = projected.shape[1]
    live_weight = (jnp.arange(seq_len, dtype=jnp.int32)[None, :] < lengths[:, None]).astype(
        jnp.float32
    ) / lengths.astype(jnp.float32)[:, None]
    left_side = projected[:, :, :proj_rank] * live_weight[:, :, None]
    right_side = projected[:, :, proj_rank:]
    outer = jnp.einsum("nsr,nsc->nrc", left_side, right_side)
    return outer.reshape(projected.shape[0], row_count * proj_rank).astype(jnp.bfloat16)


def pair_scores(train_grad, block):
    return lax.dot_general(
        train_grad, block, (((1,), (1,)), ((), ())), preferred_element_type=jnp.float32
    )


def score_against(train_grad, query_grad):
    return pair_scores(train_grad, lax.all_gather(query_grad, "dp", axis=0, tiled=True))


def per_device(
    train_inputs,
    train_grads,
    train_lengths,
    query_inputs,
    query_grads,
    query_lengths,
    proj_in,
    proj_out,
):
    whole_in, whole_out = (
        lax.all_gather(proj_in, "dp", axis=2, tiled=True),
        lax.all_gather(proj_out, "dp", axis=2, tiled=True),
    )
    half_in = whole_in[0]
    half_out = whole_out[0]
    train_part = project_tokens(train_inputs, train_grads, half_in, half_out)
    query_part = project_tokens(query_inputs, query_grads, half_in, half_out)
    proj_rank = half_in.shape[0]
    share_rows = train_inputs.shape[0] // lax.axis_size("tensor")
    core_index = lax.axis_index("tensor")
    own_lengths = lax.dynamic_slice_in_dim(train_lengths, core_index * share_rows, share_rows, 0)
    train_proj, query_proj = lax.psum((train_part, query_part), "tensor")
    own_proj = lax.dynamic_slice_in_dim(train_proj, core_index * share_rows, share_rows, 0)
    query_grad = seq_gradient(query_proj, query_lengths, proj_rank)
    return score_against(seq_gradient(own_proj, own_lengths, proj_rank), query_grad)


def solution(mesh):
    return jax.shard_map(
        per_device,
        mesh=mesh,
        in_specs=(
            P(("groups", "dp"), None, "tensor"),
            P(("groups", "dp"), None, "tensor"),
            P(("groups", "dp")),
            P(("groups", "dp"), None, "tensor"),
            P(("groups", "dp"), None, "tensor"),
            P(("groups", "dp")),
            P("tensor", None, "dp"),
            P("tensor", None, "dp"),
        ),
        out_specs=P(("groups", "dp", "tensor"), None),
        check_vma=False,
    )
```

profile of v0, /device:TPU:0, one launch (start us, length us, event | category | flops | bytes accessed | tf_op | source)
XLA Modules:
  0.0 123.3 jit_solution(17733608459283698726)
XLA Ops:
  6.5 33.3 %all_gather.10 = bf16[1,64,4096]{2,1,0:T(8,128)(2,1)S(1)} all-gather(bf16[1,64,512]{2,1,0:T(8,128)(2,1)} %param.15), channel_id=1, replica_groups=mesh['groups'=2,'dp'=8,'tensor'=2] {'dp'}, dimensions={2}, use_global_device_ids=true | all-gather | bytes 589824 | tf_op jit(solution)/shard_map/all_gather | solution.py:59
  39.9 32.7 %all_gather.9 = bf16[1,64,7168]{2,1,0:T(8,128)(2,1)S(1)} all-gather(bf16[1,64,896]{2,1,0:T(8,128)(2,1)} %param.14), channel_id=1, replica_groups=mesh['groups'=2,'dp'=8,'tensor'=2] {'dp'}, dimensions={2}, use_global_device_ids=true | all-gather | bytes 1032192 | tf_op jit(solution)/shard_map/all_gather | solution.py:58
  72.6 1.7 %fusion.6 = f32[128,64]{0,1:T(8,128)S(1)} fusion(bf16[128,4096]{1,0:T(8,128)(2,1)} %bitcast.24, bf16[1,64,4096]{2,1,0:T(8,128)(2,1)S(1)} %all_gather.10), kind=kOutput, calls=%fused_computation.8 | convolution fusion | flops 67108864 | bytes 1605632 | tf_op jit(solution)/shard_map/dot_general | solution.py:15
  74.3 0.0 copy-done
  74.3 0.0 copy-start.1
  74.3 0.8 fusion.2
  75.1 0.7 copy.13
  75.8 0.0 all-reduce.2.cloned.1.call-update
  75.8 0.0 copy-done.1
  75.8 0.1 convert_divide_fusion
  75.9 1.5 %fusion.4 = f32[96,64]{0,1:T(8,128)S(1)} fusion(bf16[96,4096]{1,0:T(8,128)(2,1)} %bitcast.25, bf16[1,64,4096]{2,1,0:T(8,128)(2,1)S(1)} %all_gather.10), kind=kOutput, calls=%fused_computation.6 | convolution fusion | flops 50331648 | bytes 1335296 | tf_op jit(solution)/shard_map/dot_general | solution.py:15
  77.5 1.9 %fusion = f32[96,64]{0,1:T(8,128)S(1)} fusion(bf16[96,7168]{1,0:T(8,128)(2,1)} %bitcast.23, bf16[1,64,7168]{2,1,0:T(8,128)(2,1)S(1)} %all_gather.9), kind=kOutput, calls=%fused_computation.2 | convolution fusion | flops 88080384 | bytes 2318336 | tf_op jit(solution)/shard_map/dot_general | solution.py:9
  79.4 0.1 copy.14
  79.5 3.5 %psum.15 = f32[3,32,128]{2,1,0:T(8,128)S(1)} all-reduce(f32[3,32,128]{2,1,0:T(8,128)S(1)} %bitcast.27), channel_id=1, replica_groups=mesh['groups'=2,'dp'=8,'tensor'=2] {'tensor'}, use_global_device_ids=true, to_apply=%region_1.0 | all-reduce | flops 12288 | bytes 98304 | tf_op jit(solution)/shard_map/psum | solution.py:69
  83.1 0.3 convolution_convert_fusion
  83.3 0.1 reshape.104
  83.5 0.1 fusion.14
  83.5 0.1 fusion.12
  83.6 30.7 %all-gather = bf16[8,3,4096]{2,1,0:T(4,128)(2,1)S(1)} all-gather(bf16[1,3,4096]{2,1,0:T(4,128)(2,1)S(1)} %reshape.104), channel_id=1, replica_groups=mesh['groups'=2,'dp'=8,'tensor'=2] {'dp'}, dimensions={0}, use_global_device_ids=true | all-gather | bytes 221184 | tf_op jit(solution)/shard_map/all_gather | solution.py:44
  114.4 0.2 reshape.105
  114.5 0.0 all-reduce.2.cloned.1.call-done
  114.6 1.1 convolution_convert_fusion.1
  115.7 0.1 convert_element_type.35
  115.8 0.7 fusion.15
  (7 shorter events, 0.0 us)
Async XLA Ops:
  6.5 67.7 %copy-start = (bf16[4,32,7168]{2,1,0:T(8,128)(2,1)S(1)}, bf16[4,32,7168]{2,1,0:T(8,128)(2,1)}, u32[]{:S(2)}) copy-start(bf16[4,32,7168]{2,1,0:T(8,128)(2,1)} %param.8) | copy-start | bytes 5505028
  6.5 108.0 %all-reduce.2.cloned.1.call-start = ((), (), s32[]{:S(2)}) async-start(), calls=%async_computation | async-start | bytes 131072 | tf_op jit(solution)/shard_map/psum | solution.py:69
  74.3 1.5 %copy-start.1 = (s32[3]{0:T(128)S(1)}, s32[3]{0:T(128)}, u32[]{:S(2)}) copy-start(s32[3]{0:T(128)} %param.13) | copy-start | bytes 40
  75.9 7.6 %copy-start.2 = (s32[4]{0:T(128)S(1)}, s32[4]{0:T(128)}, u32[]{:S(2)}) copy-start(s32[4]{0:T(128)} %param.10) | copy-start | bytes 52
Sparse Core Ops, SparseCore 0:
  75.9 19.1 all-reduce.1
where the time goes:
time: 124 us; the launch traced here: 123 us
  blocking collectives  100 us (81%)
  between operations  13.5 us (11%)
  matrix products  8.08 us (7%)
    all_gather x1, blocking collectives, per_device(): lax.all_gather(proj_out, 'dp', axis=2, tiled=True)  33.3 us
    all_gather x1, blocking collectives, per_device(): lax.all_gather(proj_in, 'dp', axis=2, tiled=True)  32.7 us
    all_gather x1, blocking collectives, score_against(): lax.all_gather(query_grad, 'dp', axis=0, tiled=True)  30.7 us
    psum x1, blocking collectives, per_device(): train_proj, query_proj = lax.psum((train_part, query_part), 'tensor')  3.53 us
    dot_general x2, matrix products, project_tokens(): lax.dot_general(grads.reshape(count, grads.shape[2]), proj_out, (((1,), (...  3.25 us
    dot_general x2, matrix products, project_tokens(): lax.dot_general(inputs.reshape(count, inputs.shape[2]), proj_in, (((1,),...  2.7 us
  transfers between devices with their start and end apart: 1, of which 0 were waited for; matrix products, arithmetic and copies ran while one was open for 4% of the time, Pallas kernels for 0%

commit v1 on v0

--- a/solution.py
+++ b/solution.py
@@ -1,7 +1,15 @@
+import functools
+
 import jax
 import jax.numpy as jnp
 from jax import lax
+from jax.experimental import pallas as pl
+from jax.experimental.pallas import tpu as pltpu
 from jax.sharding import PartitionSpec as P
+
+MESH = pl.DeviceIdType.MESH
+F32 = jnp.float32
+BF16 = jnp.bfloat16
 
 
 def project_tokens(inputs, grads, proj_in, proj_out):
@@ -44,7 +52,7 @@
     return pair_scores(train_grad, lax.all_gather(query_grad, "dp", axis=0, tiled=True))
 
 
-def per_device(
+def any_mesh(
     train_inputs,
     train_grads,
     train_lengths,
@@ -70,6 +78,297 @@
     own_proj = lax.dynamic_slice_in_dim(train_proj, core_index * share_rows, share_rows, 0)
     query_grad = seq_gradient(query_proj, query_lengths, proj_rank)
     return score_against(seq_gradient(own_proj, own_lengths, proj_rank), query_grad)
+
+
+NT = (((1,), (1,)), ((), ()))
+TN = (((0,), (0,)), ((), ()))
+
+
+def fused_kernel(
+    cfg,
+    xt_hbm, gt_hbm, lt_ref, xq_hbm, gq_hbm, lq_ref, pin_hbm, pout_hbm,
+    out_ref,
+    x_all, g_all, p_all, acc_a, acc_b, part, other, q_all, t_grad,
+    load_sem, own_sem, z_send, z_recv, x_send, x_recv, y_send, y_recv,
+    c_send, c_recv, q_send, q_recv,
+):
+    n_train, n_query, seq, rank, cin, cout, n_dp = cfg
+    n_z = n_dp // 2
+    rows_t, rows_q = n_train * seq, n_query * seq
+    half = rank // 2
+    own_t = n_train // 2
+
+    g = lax.axis_index("groups")
+    d = lax.axis_index("dp")
+    core = lax.axis_index("tensor")
+    z, x = d // 2, d % 2
+
+    own = [
+        pltpu.make_async_copy(pin_hbm, p_all.at[d, :, pl.ds(0, cin)], own_sem.at[0]),
+        pltpu.make_async_copy(pout_hbm, p_all.at[d, :, pl.ds(cin, cout)], own_sem.at[1]),
+    ]
+    loads = [
+        pltpu.make_async_copy(xt_hbm, x_all.at[pl.ds(0, rows_t)], load_sem.at[0]),
+        pltpu.make_async_copy(gt_hbm, g_all.at[pl.ds(0, rows_t)], load_sem.at[1]),
+        pltpu.make_async_copy(xq_hbm, x_all.at[pl.ds(rows_t, rows_q)], load_sem.at[2]),
+        pltpu.make_async_copy(gq_hbm, g_all.at[pl.ds(rows_t, rows_q)], load_sem.at[3]),
+    ]
+    for c in own + loads:
+        c.start()
+
+    barrier = pltpu.get_barrier_semaphore()
+    for k in range(1, n_dp):
+        pl.semaphore_signal(
+            barrier, inc=1, device_id={"dp": lax.rem(d + k, n_dp)}, device_id_type=MESH
+        )
+    pl.semaphore_signal(barrier, inc=1, device_id={"tensor": 1 - core}, device_id_type=MESH)
+    pl.semaphore_signal(barrier, inc=1, device_id={"groups": 1 - g}, device_id_type=MESH)
+    for c in own:
+        c.wait()
+    pl.semaphore_wait(barrier, n_dp + 1)
+
+    up = z // 2
+    m = z + up * (n_z - 1 - 2 * z)
+
+    def mirror(v):
+        return v + up * (n_z - 1 - 2 * v)
+
+    def z_copy(zb, zt, lane):
+        blk = p_all.at[zb * 2 + x]
+        return pltpu.make_async_remote_copy(
+            src_ref=blk, dst_ref=blk, send_sem=z_send.at[lane], recv_sem=z_recv.at[zb],
+            device_id={"dp": zt * 2 + x}, device_id_type=MESH,
+        )
+
+    def x_copy(zb, src_x):
+        blk = p_all.at[zb * 2 + src_x, pl.ds(g * half, half)]
+        return pltpu.make_async_remote_copy(
+            src_ref=blk, dst_ref=blk, send_sem=x_send.at[zb], recv_sem=x_recv.at[zb],
+            device_id={"dp": z * 2 + 1 - x}, device_id_type=MESH,
+        )
+
+    def y_copy(zb, src_g):
+        blk = p_all.at[zb * 2 + 1 - x, pl.ds(src_g * half, half)]
+        return pltpu.make_async_remote_copy(
+            src_ref=blk, dst_ref=blk, send_sem=y_send.at[zb], recv_sem=y_recv.at[zb],
+            device_id={"groups": 1 - g}, device_id_type=MESH,
+        )
+
+    zbs = [mirror(1 - m), mirror(2), mirror(3)]
+    hops = [mirror(2), mirror(0), mirror(0)]
+    first = mirror(1 - m)
+    inside = m == 1
+
+    sends = [z_copy(z, first, 0)]
+    sends[0].start()
+    inner = [z_copy(z, mirror(2), 1)]
+
+    @pl.when(inside)
+    def _():
+        inner[0].start()
+
+    xs = [x_copy(z, x)]
+    xs[0].start()
+    for c in loads:
+        c.wait()
+
+    def dots(block, start):
+        cols_in = pl.ds(pl.multiple_of(block * cin, 128), cin)
+        cols_out = pl.ds(pl.multiple_of(block * cout, 128), cout)
+        a = lax.dot_general(
+            x_all[:, cols_in], p_all[block, :, 0:cin], NT, preferred_element_type=F32
+        )
+        b = lax.dot_general(
+            g_all[:, cols_out], p_all[block, :, cin:cin + cout], NT, preferred_element_type=F32
+        )
+        if start:
+            acc_a[...] = a
+            acc_b[...] = b
+        else:
+            acc_a[...] += a
+            acc_b[...] += b
+
+    dots(d, True)
+
+    order = [z] + zbs
+    ys = []
+    for k in range(n_z):
+        if k < n_z - 1:
+            zb = zbs[k]
+            z_copy(zb, first, 0).wait_recv()
+            hop = z_copy(zb, hops[k], 2 + k)
+            inner.append(hop)
+
+            @pl.when(inside)
+            def _(hop=hop):
+                hop.start()
+
+            c = x_copy(zb, x)
+            c.start()
+            xs.append(c)
+        x_copy(order[k], 1 - x).wait_recv()
+        c = y_copy(order[k], g)
+        c.start()
+        ys.append(c)
+        if k < n_z - 1:
+            dots(zbs[k] * 2 + x, False)
+        y_copy(order[k], 1 - g).wait_recv()
+        dots(order[k] * 2 + 1 - x, False)
+
+    part[:, 0:rank] = acc_a[...]
+    part[:, rank:2 * rank] = acc_b[...]
+
+    mine = core * (own_t * seq)
+    theirs = (1 - core) * (own_t * seq)
+    cq = pltpu.make_async_remote_copy(
+        src_ref=part.at[pl.ds(rows_t, rows_q)], dst_ref=other.at[pl.ds(own_t * seq, rows_q)],
+        send_sem=c_send.at[0], recv_sem=c_recv.at[0],
+        device_id={"tensor": 1 - core}, device_id_type=MESH,
+    )
+    ct = pltpu.make_async_remote_copy(
+        src_ref=part.at[pl.ds(theirs, own_t * seq)], dst_ref=other.at[pl.ds(0, own_t * seq)],
+        send_sem=c_send.at[1], recv_sem=c_recv.at[1],
+        device_id={"tensor": 1 - core}, device_id_type=MESH,
+    )
+    cq.start()
+    ct.start()
+
+    step = lax.broadcasted_iota(jnp.int32, (seq, rank), 0)
+
+    def gradient(total, length):
+        size = jnp.broadcast_to(length, (seq, rank))
+        weight = jnp.where(step < size, 1.0, 0.0) / size.astype(F32)
+        a = total[:, 0:rank] * weight
+        b = total[:, rank:2 * rank]
+        h = lax.dot_general(
+            a, b, TN, preferred_element_type=F32, precision=lax.Precision.HIGHEST
+        ).astype(BF16)
+        return jnp.concatenate([h[0:half], h[half:rank]], axis=1)
+
+    cq.wait_recv()
+    for i in range(n_query):
+        lo = rows_t + i * seq
+        total = part[lo:lo + seq] + other[own_t * seq + i * seq:own_t * seq + (i + 1) * seq]
+        q_all[d, i * half:(i + 1) * half] = gradient(total, lq_ref[i])
+    qs = []
+    for k in range(1, n_dp):
+        c = pltpu.make_async_remote_copy(
+            src_ref=q_all.at[d], dst_ref=q_all.at[d],
+            send_sem=q_send.at[k], recv_sem=q_recv.at[d],
+            device_id={"dp": lax.rem(d + k, n_dp)}, device_id_type=MESH,
+        )
+        c.start()
+        qs.append(c)
+    ct.wait_recv()
+    for i in range(own_t):
+        total = part[pl.ds(mine + i * seq, seq)] + other[i * seq:(i + 1) * seq]
+        t_grad[i * half:(i + 1) * half] = gradient(total, lt_ref[core * own_t + i])
+
+    for k in range(1, n_dp):
+        src = lax.rem(d + k, n_dp)
+        blk = q_all.at[src]
+        pltpu.make_async_remote_copy(
+            src_ref=blk, dst_ref=blk, send_sem=q_send.at[k], recv_sem=q_recv.at[src],
+            device_id={"dp": src}, device_id_type=MESH,
+        ).wait_recv()
+
+    width = own_t * half
+    queries = n_dp * n_query
+    q_flat = q_all[...].reshape(queries * half, 2 * rank)
+    pairs = lax.dot_general(q_flat, t_grad[...], NT, preferred_element_type=F32)
+    pairs = pairs.reshape(queries, half, width)
+    row = lax.broadcasted_iota(jnp.int32, (queries, half, width), 1)
+    col = lax.broadcasted_iota(jnp.int32, (queries, half, width), 2) % half
+    diag = jnp.sum(jnp.where(row == col, pairs, 0.0), axis=1)
+    pick = (
+        lax.broadcasted_iota(jnp.int32, (own_t, width), 1) // half
+        == lax.broadcasted_iota(jnp.int32, (own_t, width), 0)
+    ).astype(F32)
+    out_ref[...] = lax.dot_general(
+        pick, diag, NT, preferred_element_type=F32, precision=lax.Precision.HIGHEST
+    )
+
+    for c in sends + xs + ys + [cq, ct] + qs:
+        c.wait_send()
+
+    @pl.when(inside)
+    def _():
+        for c in inner:
+            c.wait_send()
+
+
+def fused(
+    train_inputs, train_grads, train_lengths, query_inputs, query_grads, query_lengths,
+    proj_in, proj_out,
+):
+    n_dp = lax.axis_size("dp")
+    n_train, seq, win = train_inputs.shape
+    n_query, _, wout = query_grads.shape
+    _, rank, cin = proj_in.shape
+    cout = proj_out.shape[2]
+    rows_t, rows_q = n_train * seq, n_query * seq
+    rows = rows_t + rows_q
+    half = rank // 2
+    own_t = n_train // 2
+    cfg = (n_train, n_query, seq, rank, cin, cout, n_dp)
+    hbm = pl.BlockSpec(memory_space=pl.ANY)
+    smem = pl.BlockSpec(memory_space=pltpu.SMEM)
+    dma = pltpu.SemaphoreType.DMA
+    return pl.pallas_call(
+        functools.partial(fused_kernel, cfg),
+        out_shape=jax.ShapeDtypeStruct((own_t, n_dp * n_query), F32),
+        in_specs=[hbm, hbm, smem, hbm, hbm, smem, hbm, hbm],
+        out_specs=pl.BlockSpec(memory_space=pltpu.VMEM),
+        scratch_shapes=[
+            pltpu.VMEM((rows, win), BF16),
+            pltpu.VMEM((rows, wout), BF16),
+            pltpu.VMEM((n_dp, rank, cin + cout), BF16),
+            pltpu.VMEM((rows, rank), F32),
+            pltpu.VMEM((rows, rank), F32),
+            pltpu.VMEM((rows, 2 * rank), F32),
+            pltpu.VMEM((own_t * seq + rows_q, 2 * rank), F32),
+            pltpu.VMEM((n_dp, n_query * half, 2 * rank), BF16),
+            pltpu.VMEM((own_t * half, 2 * rank), BF16),
+            dma((4,)),
+            dma((2,)),
+            dma((5,)),
+            dma((4,)),
+            dma((4,)),
+            dma((4,)),
+            dma((4,)),
+            dma((4,)),
+            dma((2,)),
+            dma((2,)),
+            dma((n_dp,)),
+            dma((n_dp,)),
+        ],
+        compiler_params=pltpu.CompilerParams(
+            collective_id=0, has_side_effects=True, vmem_limit_bytes=40 * 1024 * 1024
+        ),
+    )(
+        train_inputs.reshape(rows_t, win),
+        train_grads.reshape(rows_t, wout),
+        train_lengths,
+        query_inputs.reshape(rows_q, win),
+        query_grads.reshape(rows_q, wout),
+        query_lengths,
+        proj_in[0],
+        proj_out[0],
+    )
+
+
+def per_device(*args):
+    proj_in, proj_out = args[6], args[7]
+    sizes = (lax.axis_size("groups"), lax.axis_size("dp"), lax.axis_size("tensor"))
+    fits = (
+        sizes == (2, 8, 2)
+        and proj_in.shape[2] % 128 == 0
+        and proj_out.shape[2] % 128 == 0
+        and proj_in.shape[1] == 64
+        and args[0].shape[0] % 2 == 0
+        and args[0].shape[1] % 16 == 0
+    )
+    return fused(*args) if fits else any_mesh(*args)
 
 
 def solution(mesh):

time: 124 us -> 48.8 us (0.39)
  the two profiles are of different devices: /device:TPU:0 before, /device:TPU:1 now
where the time goes in v1:
time: 48.8 us; the launch traced here: 47.9 us
  Pallas kernels  39 us (80%)
  local copies, waits for them, and re-layouts  8.81 us (18%)
    pallas_call x1, Pallas kernels, fused(): pl.pallas_call(functools.partial(fused_kernel, cfg), out_shape=jax.ShapeD...  39 us
    unnamed x17, local copies, waits for them, and re-layouts  8.81 us

profile of v1, /device:TPU:1, one launch (start us, length us, event | category | flops | bytes accessed | tf_op | source)
XLA Modules:
  0.0 47.9 jit_solution(10392018687225952468)
XLA Ops:
  0.0 0.0 copy-start
  0.0 1.5 %copy-done = bf16[4,32,7168]{2,1,0:T(8,128)(2,1)S(1)} copy-done((bf16[4,32,7168]{2,1,0:T(8,128)(2,1)S(1)}, bf16[4,32,7168]{2,1,0:T(8,128)(2,1)}, u32[]{:S(2)}) %copy-start) | copy-done | bytes 1835032
  1.5 0.0 copy-start.1
  1.5 1.3 %copy-done.1 = bf16[3,32,7168]{2,1,0:T(8,128)(2,1)S(1)} copy-done((bf16[3,32,7168]{2,1,0:T(8,128)(2,1)S(1)}, bf16[3,32,7168]{2,1,0:T(8,128)(2,1)}, u32[]{:S(2)}) %copy-start.1) | copy-done | bytes 1376280
  2.8 0.0 copy-start.2
  2.8 1.2 %copy-done.2 = bf16[4,32,4096]{2,1,0:T(8,128)(2,1)S(1)} copy-done((bf16[4,32,4096]{2,1,0:T(8,128)(2,1)S(1)}, bf16[4,32,4096]{2,1,0:T(8,128)(2,1)}, u32[]{:S(2)}) %copy-start.2) | copy-done | bytes 1048600
  4.1 0.0 copy-start.3
  4.1 1.1 %copy-done.3 = bf16[3,32,4096]{2,1,0:T(8,128)(2,1)S(1)} copy-done((bf16[3,32,4096]{2,1,0:T(8,128)(2,1)S(1)}, bf16[3,32,4096]{2,1,0:T(8,128)(2,1)}, u32[]{:S(2)}) %copy-start.3) | copy-done | bytes 786456
  5.2 0.0 copy-start.4
  5.2 0.9 %copy-done.4 = bf16[1,64,896]{2,1,0:T(8,128)(2,1)S(1)} copy-done((bf16[1,64,896]{2,1,0:T(8,128)(2,1)S(1)}, bf16[1,64,896]{2,1,0:T(8,128)(2,1)}, u32[]{:S(2)}) %copy-start.4) | copy-done | bytes 114712
  6.1 0.0 copy-start.5
  6.1 0.8 %copy-done.5 = bf16[1,64,512]{2,1,0:T(8,128)(2,1)S(1)} copy-done((bf16[1,64,512]{2,1,0:T(8,128)(2,1)S(1)}, bf16[1,64,512]{2,1,0:T(8,128)(2,1)}, u32[]{:S(2)}) %copy-start.5) | copy-done | bytes 65560
  6.9 0.0 copy-start.6
  6.9 0.7 %copy-done.6 = s32[4]{0:T(128)S(1)} copy-done((s32[4]{0:T(128)S(1)}, s32[4]{0:T(128)}, u32[]{:S(2)}) %copy-start.6) | copy-done | bytes 40
  7.6 0.0 copy-start.7
  7.6 0.7 %copy-done.7 = s32[3]{0:T(128)S(1)} copy-done((s32[3]{0:T(128)S(1)}, s32[3]{0:T(128)}, u32[]{:S(2)}) %copy-start.7) | copy-done | bytes 36
  8.2 39.0 %shard_map.82 = f32[2,24]{1,0:T(2,128)S(1)} custom-call(bf16[128,7168]{1,0:T(8,128)(2,1)S(1)} %bitcast.6, bf16[128,4096]{1,0:T(8,128)(2,1)S(1)} %bitcast.8, s32[4]{0:T(128)S(1)} %copy-done.6, bf16[96,7168]{1,0:T(8,128)(2,1)S(1)} %bitcast.7, bf16[96,4096]{1,0:T(8,128)(2,1)S(1)} %bitcast.9, s32[3]{0:T(128)S(1)} %copy-done.7, bf16[64,896]{1,0:T(8,128)(2,1)S(1)} %bitcast.10, ...), custom_call_target="tpu_custom_call" | custom-call | tf_op jit(solution)/shard_map/pallas_call | solution.py:317
  47.3 0.6 %copy.10 = f32[2,24]{1,0:T(2,128)} copy(f32[2,24]{1,0:T(2,128)S(1)} %shard_map.82) | data formatting | bytes 384
Async XLA Ops:
  0.0 1.5 %copy-start = (bf16[4,32,7168]{2,1,0:T(8,128)(2,1)S(1)}, bf16[4,32,7168]{2,1,0:T(8,128)(2,1)}, u32[]{:S(2)}) copy-start(bf16[4,32,7168]{2,1,0:T(8,128)(2,1)} %param.8) | copy-start | bytes 5505028
  1.5 1.3 %copy-start.1 = (bf16[3,32,7168]{2,1,0:T(8,128)(2,1)S(1)}, bf16[3,32,7168]{2,1,0:T(8,128)(2,1)}, u32[]{:S(2)}) copy-start(bf16[3,32,7168]{2,1,0:T(8,128)(2,1)} %param.11) | copy-start | bytes 4128772
  2.8 1.2 %copy-start.2 = (bf16[4,32,4096]{2,1,0:T(8,128)(2,1)S(1)}, bf16[4,32,4096]{2,1,0:T(8,128)(2,1)}, u32[]{:S(2)}) copy-start(bf16[4,32,4096]{2,1,0:T(8,128)(2,1)} %param.9) | copy-start | bytes 3145732
  4.1 1.1 %copy-start.3 = (bf16[3,32,4096]{2,1,0:T(8,128)(2,1)S(1)}, bf16[3,32,4096]{2,1,0:T(8,128)(2,1)}, u32[]{:S(2)}) copy-start(bf16[3,32,4096]{2,1,0:T(8,128)(2,1)} %param.12) | copy-start | bytes 2359300
  5.2 0.9 %copy-start.4 = (bf16[1,64,896]{2,1,0:T(8,128)(2,1)S(1)}, bf16[1,64,896]{2,1,0:T(8,128)(2,1)}, u32[]{:S(2)}) copy-start(bf16[1,64,896]{2,1,0:T(8,128)(2,1)} %param.14) | copy-start | bytes 344068
  6.1 0.8 %copy-start.5 = (bf16[1,64,512]{2,1,0:T(8,128)(2,1)S(1)}, bf16[1,64,512]{2,1,0:T(8,128)(2,1)}, u32[]{:S(2)}) copy-start(bf16[1,64,512]{2,1,0:T(8,128)(2,1)} %param.15) | copy-start | bytes 196612
  6.9 0.7 %copy-start.6 = (s32[4]{0:T(128)S(1)}, s32[4]{0:T(128)}, u32[]{:S(2)}) copy-start(s32[4]{0:T(128)} %lt_ref.1) | copy-start | bytes 52
  7.6 0.7 %copy-start.7 = (s32[3]{0:T(128)S(1)}, s32[3]{0:T(128)}, u32[]{:S(2)}) copy-start(s32[3]{0:T(128)} %lq_ref.1) | copy-start | bytes 40

commit v2 on v1

--- a/solution.py
+++ b/solution.py
@@ -86,9 +86,9 @@
 
 def fused_kernel(
     cfg,
-    xt_hbm, gt_hbm, lt_ref, xq_hbm, gq_hbm, lq_ref, pin_hbm, pout_hbm,
+    xt_hbm, gt_hbm, lt_hbm, xq_hbm, gq_hbm, lq_hbm, pin_hbm, pout_hbm,
     out_ref,
-    x_all, g_all, p_all, acc_a, acc_b, part, other, q_all, t_grad,
+    lt_ref, lq_ref, x_all, g_all, p_all, acc_a, acc_b, part, other, q_all, t_grad,
     load_sem, own_sem, z_send, z_recv, x_send, x_recv, y_send, y_recv,
     c_send, c_recv, q_send, q_recv,
 ):
@@ -112,6 +112,8 @@
         pltpu.make_async_copy(gt_hbm, g_all.at[pl.ds(0, rows_t)], load_sem.at[1]),
         pltpu.make_async_copy(xq_hbm, x_all.at[pl.ds(rows_t, rows_q)], load_sem.at[2]),
         pltpu.make_async_copy(gq_hbm, g_all.at[pl.ds(rows_t, rows_q)], load_sem.at[3]),
+        pltpu.make_async_copy(lt_hbm, lt_ref, load_sem.at[4]),
+        pltpu.make_async_copy(lq_hbm, lq_ref, load_sem.at[5]),
     ]
     for c in own + loads:
         c.start()
@@ -133,10 +135,12 @@
     def mirror(v):
         return v + up * (n_z - 1 - 2 * v)
 
-    def z_copy(zb, zt, lane):
-        blk = p_all.at[zb * 2 + x]
+    def z_copy(zb, zt, part_no, lane):
+        rows = (g if part_no == 0 else 1 - g) * half
+        blk = p_all.at[zb * 2 + x, pl.ds(rows, half)]
         return pltpu.make_async_remote_copy(
-            src_ref=blk, dst_ref=blk, send_sem=z_send.at[lane], recv_sem=z_recv.at[zb],
+            src_ref=blk, dst_ref=blk,
+            send_sem=z_send.at[2 * lane + part_no], recv_sem=z_recv.at[2 * zb + part_no],
             device_id={"dp": zt * 2 + x}, device_id_type=MESH,
         )
 
@@ -159,16 +163,23 @@
     first = mirror(1 - m)
     inside = m == 1
 
-    sends = [z_copy(z, first, 0)]
-    sends[0].start()
-    inner = [z_copy(z, mirror(2), 1)]
-
-    @pl.when(inside)
-    def _():
-        inner[0].start()
-
-    xs = [x_copy(z, x)]
-    xs[0].start()
+    sends, inner, xs, ys = [], [], [], []
+
+    def send_inner(copy):
+        inner.append(copy)
+
+        @pl.when(inside)
+        def _():
+            copy.start()
+
+    for part_no in range(2):
+        c = z_copy(z, first, part_no, 0)
+        c.start()
+        sends.append(c)
+        send_inner(z_copy(z, mirror(2), part_no, 1))
+        if part_no == 0:
+            xs.append(x_copy(z, x))
+            xs[0].start()
     for c in loads:
         c.wait()
 
@@ -191,29 +202,33 @@
     dots(d, True)
 
     order = [z] + zbs
-    ys = []
-    for k in range(n_z):
-        if k < n_z - 1:
-            zb = zbs[k]
-            z_copy(zb, first, 0).wait_recv()
-            hop = z_copy(zb, hops[k], 2 + k)
-            inner.append(hop)
-
-            @pl.when(inside)
-            def _(hop=hop):
-                hop.start()
-
-            c = x_copy(zb, x)
-            c.start()
-            xs.append(c)
+
+    def hand_on(k):
         x_copy(order[k], 1 - x).wait_recv()
         c = y_copy(order[k], g)
         c.start()
         ys.append(c)
-        if k < n_z - 1:
-            dots(zbs[k] * 2 + x, False)
+
+    def finish(k):
         y_copy(order[k], 1 - g).wait_recv()
         dots(order[k] * 2 + 1 - x, False)
+
+    for k in range(n_z - 1):
+        zb = zbs[k]
+        z_copy(zb, first, 0, 0).wait_recv()
+        send_inner(z_copy(zb, hops[k], 0, 2 + k))
+        c = x_copy(zb, x)
+        c.start()
+        xs.append(c)
+        hand_on(k)
+        z_copy(zb, first, 1, 0).wait_recv()
+        send_inner(z_copy(zb, hops[k], 1, 2 + k))
+        dots(zb * 2 + x, False)
+        if k >= 1:
+            finish(k - 1)
+    hand_on(n_z - 1)
+    finish(n_z - 2)
+    finish(n_z - 1)
 
     part[:, 0:rank] = acc_a[...]
     part[:, rank:2 * rank] = acc_b[...]
@@ -311,15 +326,16 @@
     half = rank // 2
     own_t = n_train // 2
     cfg = (n_train, n_query, seq, rank, cin, cout, n_dp)
-    hbm = pl.BlockSpec(memory_space=pl.ANY)
-    smem = pl.BlockSpec(memory_space=pltpu.SMEM)
+    hbm = pl.BlockSpec(memory_space=pltpu.HBM)
     dma = pltpu.SemaphoreType.DMA
     return pl.pallas_call(
         functools.partial(fused_kernel, cfg),
         out_shape=jax.ShapeDtypeStruct((own_t, n_dp * n_query), F32),
-        in_specs=[hbm, hbm, smem, hbm, hbm, smem, hbm, hbm],
+        in_specs=[hbm] * 8,
         out_specs=pl.BlockSpec(memory_space=pltpu.VMEM),
         scratch_shapes=[
+            pltpu.SMEM((n_train,), jnp.int32),
+            pltpu.SMEM((n_query,), jnp.int32),
             pltpu.VMEM((rows, win), BF16),
             pltpu.VMEM((rows, wout), BF16),
             pltpu.VMEM((n_dp, rank, cin + cout), BF16),
@@ -329,10 +345,10 @@
             pltpu.VMEM((own_t * seq + rows_q, 2 * rank), F32),
             pltpu.VMEM((n_dp, n_query * half, 2 * rank), BF16),
             pltpu.VMEM((own_t * half, 2 * rank), BF16),
-            dma((4,)),
+            dma((6,)),
             dma((2,)),
-            dma((5,)),
-            dma((4,)),
+            dma((10,)),
+            dma((8,)),
             dma((4,)),
             dma((4,)),
             dma((4,)),
@@ -343,7 +359,7 @@
             dma((n_dp,)),
         ],
         compiler_params=pltpu.CompilerParams(
-            collective_id=0, has_side_effects=True, vmem_limit_bytes=40 * 1024 * 1024
+            collective_id=0, has_side_effects=True, vmem_limit_bytes=64 * 1024 * 1024
         ),
     )(
         train_inputs.reshape(rows_t, win),

time: 48.8 us -> 35.4 us (0.73); the launches traced: 47.9 us -> 35.3 us
  local copies, waits for them, and re-layouts: 8.81 us -> 1.24 us
  Pallas kernels: 39 us -> 34 us
    unnamed x17 -> x1, local copies, waits for them, and re-layouts: 8.81 us -> 1.24 us
    pallas_call x1, Pallas kernels: 39 us -> 34 us  [fused(): pl.pallas_call(functools.partial(fused_kernel, cfg), out_shape=jax.ShapeD...]
where the time goes in v2:
time: 35.4 us; the launch traced here: 35.3 us
  Pallas kernels  34 us (96%)
  local copies, waits for them, and re-layouts  1.24 us (4%)
    pallas_call x1, Pallas kernels, fused(): pl.pallas_call(functools.partial(fused_kernel, cfg), out_shape=jax.ShapeD...  34 us
    unnamed x1, local copies, waits for them, and re-layouts  1.24 us

profile of v2, /device:TPU:1, one launch (start us, length us, event | category | flops | bytes accessed | tf_op | source)
XLA Modules:
  0.0 35.3 jit_solution(7732901012263373304)
XLA Ops:
  0.0 34.0 %shard_map.82 = f32[2,24]{1,0:T(2,128)} custom-call(bf16[128,7168]{1,0:T(8,128)(2,1)} %bitcast.6, bf16[128,4096]{1,0:T(8,128)(2,1)} %bitcast.8, s32[4]{0:T(128)} %lt_hbm.1, bf16[96,7168]{1,0:T(8,128)(2,1)} %bitcast.7, bf16[96,4096]{1,0:T(8,128)(2,1)} %bitcast.9, s32[3]{0:T(128)} %lq_hbm.1, bf16[64,896]{1,0:T(8,128)(2,1)} %bitcast.10, bf16[64,512]{1,0:T(8,128)(2,1)} %bitcast.11), custom_call_target="tpu_custom_call" | custom-call | tf_op jit(solution)/shard_map/pallas_call | solution.py:331
  34.0 1.2 %copy.10 = f32[2,24]{1,0:T(2,128)} copy(f32[2,24]{1,0:T(2,128)} %shard_map.82) | data formatting | bytes 384

commit v3 on v2

--- a/solution.py
+++ b/solution.py
@@ -115,25 +115,37 @@
         pltpu.make_async_copy(lt_hbm, lt_ref, load_sem.at[4]),
         pltpu.make_async_copy(lq_hbm, lq_ref, load_sem.at[5]),
     ]
-    for c in own + loads:
-        c.start()
+    for c in own:
+        c.start()
+
+    up = z // 2
+    m = z + up * (n_z - 1 - 2 * z)
+
+    def mirror(v):
+        return v + up * (n_z - 1 - 2 * v)
+
+    first = mirror(1 - m)
+    inside = m == 1
 
     barrier = pltpu.get_barrier_semaphore()
-    for k in range(1, n_dp):
+    pl.semaphore_signal(
+        barrier, inc=1, device_id={"dp": first * 2 + x}, device_id_type=MESH
+    )
+
+    @pl.when(inside)
+    def _():
         pl.semaphore_signal(
-            barrier, inc=1, device_id={"dp": lax.rem(d + k, n_dp)}, device_id_type=MESH
-        )
+            barrier, inc=1, device_id={"dp": mirror(2) * 2 + x}, device_id_type=MESH
+        )
+
+    pl.semaphore_signal(barrier, inc=1, device_id={"dp": z * 2 + 1 - x}, device_id_type=MESH)
     pl.semaphore_signal(barrier, inc=1, device_id={"tensor": 1 - core}, device_id_type=MESH)
     pl.semaphore_signal(barrier, inc=1, device_id={"groups": 1 - g}, device_id_type=MESH)
     for c in own:
         c.wait()
-    pl.semaphore_wait(barrier, n_dp + 1)
-
-    up = z // 2
-    m = z + up * (n_z - 1 - 2 * z)
-
-    def mirror(v):
-        return v + up * (n_z - 1 - 2 * v)
+    for c in loads:
+        c.start()
+    pl.semaphore_wait(barrier, 4 + m)
 
     def z_copy(zb, zt, part_no, lane):
         rows = (g if part_no == 0 else 1 - g) * half
@@ -160,8 +172,6 @@
 
     zbs = [mirror(1 - m), mirror(2), mirror(3)]
     hops = [mirror(2), mirror(0), mirror(0)]
-    first = mirror(1 - m)
-    inside = m == 1
 
     sends, inner, xs, ys = [], [], [], []
 
@@ -172,16 +182,15 @@
         def _():
             copy.start()
 
-    for part_no in range(2):
+    def send_own(part_no):
         c = z_copy(z, first, part_no, 0)
         c.start()
         sends.append(c)
         send_inner(z_copy(z, mirror(2), part_no, 1))
-        if part_no == 0:
-            xs.append(x_copy(z, x))
-            xs[0].start()
-    for c in loads:
-        c.wait()
+
+    send_own(0)
+    xs.append(x_copy(z, x))
+    xs[0].start()
 
     def dots(block, start):
         cols_in = pl.ds(pl.multiple_of(block * cin, 128), cin)
@@ -199,8 +208,6 @@
             acc_a[...] += a
             acc_b[...] += b
 
-    dots(d, True)
-
     order = [z] + zbs
 
     def hand_on(k):
@@ -220,15 +227,22 @@
         c = x_copy(zb, x)
         c.start()
         xs.append(c)
+        if k == 0:
+            send_own(1)
         hand_on(k)
+        if k == 0:
+            for c in loads:
+                c.wait()
+            dots(d, True)
+    finish(0)
+    for k in range(n_z - 1):
+        zb = zbs[k]
         z_copy(zb, first, 1, 0).wait_recv()
         send_inner(z_copy(zb, hops[k], 1, 2 + k))
+        if k == 0:
+            hand_on(n_z - 1)
         dots(zb * 2 + x, False)
-        if k >= 1:
-            finish(k - 1)
-    hand_on(n_z - 1)
-    finish(n_z - 2)
-    finish(n_z - 1)
+        finish(k + 1)
 
     part[:, 0:rank] = acc_a[...]
     part[:, rank:2 * rank] = acc_b[...]

time: 35.4 us -> 31.5 us (0.89)
  Pallas kernels: 34 us -> 30.1 us
    pallas_call x1, Pallas kernels: 34 us -> 30.1 us  [fused(): pl.pallas_call(functools.partial(fused_kernel, cfg), out_shape=jax.ShapeD...]
where the time goes in v3:
time: 31.5 us; the launch traced here: 31.3 us
  Pallas kernels  30.1 us (96%)
  local copies, waits for them, and re-layouts  1.24 us (4%)
    pallas_call x1, Pallas kernels, fused(): pl.pallas_call(functools.partial(fused_kernel, cfg), out_shape=jax.ShapeD...  30.1 us
    unnamed x1, local copies, waits for them, and re-layouts  1.24 us

profile of v3, /device:TPU:1, one launch (start us, length us, event | category | flops | bytes accessed | tf_op | source)
XLA Modules:
  0.0 31.3 jit_solution(8806608027881086565)
XLA Ops:
  0.0 30.1 %shard_map.82 = f32[2,24]{1,0:T(2,128)} custom-call(bf16[128,7168]{1,0:T(8,128)(2,1)} %bitcast.6, bf16[128,4096]{1,0:T(8,128)(2,1)} %bitcast.8, s32[4]{0:T(128)} %lt_hbm.1, bf16[96,7168]{1,0:T(8,128)(2,1)} %bitcast.7, bf16[96,4096]{1,0:T(8,128)(2,1)} %bitcast.9, s32[3]{0:T(128)} %lq_hbm.1, bf16[64,896]{1,0:T(8,128)(2,1)} %bitcast.10, bf16[64,512]{1,0:T(8,128)(2,1)} %bitcast.11), custom_call_target="tpu_custom_call" | custom-call | tf_op jit(solution)/shard_map/pallas_call | solution.py:345
  30.1 1.2 %copy.10 = f32[2,24]{1,0:T(2,128)} copy(f32[2,24]{1,0:T(2,128)} %shard_map.82) | data formatting | bytes 384

commit v4 on v3

--- a/solution.py
+++ b/solution.py
@@ -95,7 +95,7 @@
     n_train, n_query, seq, rank, cin, cout, n_dp = cfg
     n_z = n_dp // 2
     rows_t, rows_q = n_train * seq, n_query * seq
-    half = rank // 2
+    half, quarter = rank // 2, rank // 4
     own_t = n_train // 2
 
     g = lax.axis_index("groups")
@@ -156,17 +156,17 @@
             device_id={"dp": zt * 2 + x}, device_id_type=MESH,
         )
 
-    def x_copy(zb, src_x):
-        blk = p_all.at[zb * 2 + src_x, pl.ds(g * half, half)]
+    def x_copy(zb, src_x, piece):
+        blk = p_all.at[zb * 2 + src_x, pl.ds(g * half + piece * quarter, quarter)]
         return pltpu.make_async_remote_copy(
-            src_ref=blk, dst_ref=blk, send_sem=x_send.at[zb], recv_sem=x_recv.at[zb],
+            src_ref=blk, dst_ref=blk, send_sem=x_send.at[2 * zb + piece], recv_sem=x_recv.at[2 * zb + piece],
             device_id={"dp": z * 2 + 1 - x}, device_id_type=MESH,
         )
 
-    def y_copy(zb, src_g):
-        blk = p_all.at[zb * 2 + 1 - x, pl.ds(src_g * half, half)]
+    def y_copy(zb, src_g, piece):
+        blk = p_all.at[zb * 2 + 1 - x, pl.ds(src_g * half + piece * quarter, quarter)]
         return pltpu.make_async_remote_copy(
-            src_ref=blk, dst_ref=blk, send_sem=y_send.at[zb], recv_sem=y_recv.at[zb],
+            src_ref=blk, dst_ref=blk, send_sem=y_send.at[2 * zb + piece], recv_sem=y_recv.at[2 * zb + piece],
             device_id={"groups": 1 - g}, device_id_type=MESH,
         )
 
@@ -181,6 +181,12 @@
         @pl.when(inside)
         def _():
             copy.start()
+
+    def send_x(zb):
+        for piece in range(2):
+            c = x_copy(zb, x, piece)
+            c.start()
+            xs.append(c)
 
     def send_own(part_no):
         c = z_copy(z, first, part_no, 0)
@@ -189,8 +195,7 @@
         send_inner(z_copy(z, mirror(2), part_no, 1))
 
     send_own(0)
-    xs.append(x_copy(z, x))
-    xs[0].start()
+    send_x(z)
 
     def dots(block, start):
         cols_in = pl.ds(pl.multiple_of(block * cin, 128), cin)
@@ -211,22 +216,22 @@
     order = [z] + zbs
 
     def hand_on(k):
-        x_copy(order[k], 1 - x).wait_recv()
-        c = y_copy(order[k], g)
-        c.start()
-        ys.append(c)
+        for piece in range(2):
+            x_copy(order[k], 1 - x, piece).wait_recv()
+            c = y_copy(order[k], g, piece)
+            c.start()
+            ys.append(c)
 
     def finish(k):
-        y_copy(order[k], 1 - g).wait_recv()
+        for piece in range(2):
+            y_copy(order[k], 1 - g, piece).wait_recv()
         dots(order[k] * 2 + 1 - x, False)
 
     for k in range(n_z - 1):
         zb = zbs[k]
         z_copy(zb, first, 0, 0).wait_recv()
         send_inner(z_copy(zb, hops[k], 0, 2 + k))
-        c = x_copy(zb, x)
-        c.start()
-        xs.append(c)
+        send_x(zb)
         if k == 0:
             send_own(1)
         hand_on(k)
@@ -363,10 +368,10 @@
             dma((2,)),
             dma((10,)),
             dma((8,)),
-            dma((4,)),
-            dma((4,)),
-            dma((4,)),
-            dma((4,)),
+            dma((8,)),
+            dma((8,)),
+            dma((9,)),
+            dma((9,)),
             dma((2,)),
             dma((2,)),
             dma((n_dp,)),

time: 31.5 us -> 31.1 us (0.987)
  Pallas kernels: 30.1 us -> 29.7 us
where the time goes in v4:
time: 31.1 us; the launch traced here: 31 us
  Pallas kernels  29.7 us (95%)
  local copies, waits for them, and re-layouts  1.24 us (4%)
    pallas_call x1, Pallas kernels, fused(): pl.pallas_call(functools.partial(fused_kernel, cfg), out_shape=jax.ShapeD...  29.7 us
    unnamed x1, local copies, waits for them, and re-layouts  1.24 us

profile of v4, /device:TPU:1, one launch (start us, length us, event | category | flops | bytes accessed | tf_op | source)
XLA Modules:
  0.0 31.0 jit_solution(8147943908911371605)
XLA Ops:
  0.0 29.7 %shard_map.82 = f32[2,24]{1,0:T(2,128)} custom-call(bf16[128,7168]{1,0:T(8,128)(2,1)} %bitcast.6, bf16[128,4096]{1,0:T(8,128)(2,1)} %bitcast.8, s32[4]{0:T(128)} %lt_hbm.1, bf16[96,7168]{1,0:T(8,128)(2,1)} %bitcast.7, bf16[96,4096]{1,0:T(8,128)(2,1)} %bitcast.9, s32[3]{0:T(128)} %lq_hbm.1, bf16[64,896]{1,0:T(8,128)(2,1)} %bitcast.10, bf16[64,512]{1,0:T(8,128)(2,1)} %bitcast.11), custom_call_target="tpu_custom_call" | custom-call | tf_op jit(solution)/shard_map/pallas_call | solution.py:350
  29.8 1.2 %copy.10 = f32[2,24]{1,0:T(2,128)} copy(f32[2,24]{1,0:T(2,128)} %shard_map.82) | data formatting | bytes 384
